TPU v7x, 32 devices: a whole 2x2x4 slice. The times are simulated.
32 devices in a mesh: row: 2 (over y), col: 16 (over z, x, core).
Axes of the slice: x: 2, y: 2, z: 4, core: 2. Of those that a mesh axis runs over, the one named last changes fastest.
Arguments:
- coefficients: float32 [2, 2, 8, 2048, 512], P(None, None, None, ('row', 'col')), may hold values from -6 to 6
- vertical_modes: float32 [512, 512], replicated, may hold values from -0.25 to 0.25
- mode_slopes: float32 [512, 512], replicated, may hold values from -0.25 to 0.25
- dual_modes: float32 [512, 512], replicated, may hold values from -0.25 to 0.25
- eigenvalues: float32 [512], replicated, may hold values from 0.01 to 10
- velocity: float32 [3, 512, 2048], P(None, 'col'), may hold values from -5 to 5
- gradient: float32 [2, 512], P(None, 'col'), may hold values from 0.2 to 2
- span_wavenumbers: float32 [8], replicated, may hold values from 0 to 2
- implicit_rates: float32 [2], replicated, may hold values from 0.02 to 0.2
- time_step: float32 [], replicated, may hold values from 0.2 to 0.5
Outputs:
- new_coefficients: float32 [2, 2, 8, 2048, 512], P(None, None, None, ('row', 'col'))
All inputs are finite; a program needn't handle non-finite values.
Results may differ from a plain program's by a relative error of at most 0.00005.
Values sent between devices are 32-bit elements; how exact they have to be, the bound alone decides.
A program may use at most 128 MiB of HBM per device.

v0:
```python
import math
import jax
import jax.numpy as jnp
from jax import lax
from jax.sharding import PartitionSpec as P

highest = lax.Precision.HIGHEST
lane_width = 128


def signed_waves(length):
    indices = jnp.arange(length, dtype=jnp.int32)
    return jnp.where(indices < length // 2, indices, indices - length)


def phase_table(row_total, col_total, period, direction):
    left_index = jnp.arange(row_total, dtype=jnp.int32)[:, None]
    right_index = jnp.arange(col_total, dtype=jnp.int32)[None, :]
    angles = (left_index * right_index % period).astype(jnp.float32) * (2.0 * math.pi / period)
    return (jnp.cos(angles), direction * jnp.sin(angles))


def contract(form, left_real, left_imag, right_real, right_imag):
    product_real = jnp.einsum(form, left_real, right_real, precision=highest) - jnp.einsum(
        form, left_imag, right_imag, precision=highest
    )
    product_imag = jnp.einsum(form, left_real, right_imag, precision=highest) + jnp.einsum(
        form, left_imag, right_real, precision=highest
    )
    return (product_real, product_imag)


def twisted(real_in, imag_in, twist_real, twist_imag):
    return (
        real_in * twist_real - imag_in * twist_imag,
        real_in * twist_imag + imag_in * twist_real,
    )


def inverse_transform(real_in, imag_in, length):
    short_size = length // lane_width
    scale = 1.0 / math.sqrt(length)
    short_real, short_imag = phase_table(short_size, short_size, short_size, 1.0)
    twist_real, twist_imag = phase_table(short_size, lane_width, length, 1.0)
    wide_real, wide_imag = phase_table(lane_width, lane_width, lane_width, 1.0)
    middle_real, middle_imag = contract("...ef,ed->...df", real_in, imag_in, short_real, short_imag)
    middle_real, middle_imag = twisted(middle_real, middle_imag, twist_real, twist_imag)
    return contract(
        "...df,fc->...dc", middle_real, middle_imag, wide_real * scale, wide_imag * scale
    )


def forward_transform(real_in, imag_in, length):
    short_size = length // lane_width
    scale = 1.0 / math.sqrt(length)
    short_real, short_imag = phase_table(short_size, short_size, short_size, -1.0)
    twist_real, twist_imag = phase_table(short_size, lane_width, length, -1.0)
    wide_real, wide_imag = phase_table(lane_width, lane_width, lane_width, -1.0)
    middle_real, middle_imag = contract("...dc,cf->...df", real_in, imag_in, wide_real, wide_imag)
    middle_real, middle_imag = twisted(middle_real, middle_imag, twist_real, twist_imag)
    return contract(
        "...df,de->...ef", middle_real, middle_imag, short_real * scale, short_imag * scale
    )


def on_device(
    coefficients,
    vertical_modes,
    mode_slopes,
    dual_modes,
    eigenvalues,
    velocity,
    gradient,
    span_wavenumbers,
    implicit_rates,
    time_step,
):
    row_count = lax.axis_size("row")
    col_count = lax.axis_size("col")
    local_waves = coefficients.shape[3]
    total_points = local_waves * row_count * col_count
    short_size = total_points // lane_width
    first_wave = (lax.axis_index("row") * col_count + lax.axis_index("col")) * local_waves
    signed = signed_waves(total_points)
    zonal_waves = signed.astype(jnp.float32) * (2.0 * math.pi / total_points)
    own_waves = lax.dynamic_slice_in_dim(zonal_waves, first_wave, local_waves)
    value_real = jnp.einsum("sqpj,zj->zsqp", coefficients[:, 0], vertical_modes, precision=highest)
    value_imag = jnp.einsum("sqpj,zj->zsqp", coefficients[:, 1], vertical_modes, precision=highest)
    slope_real = jnp.einsum("sqpj,zj->zsqp", coefficients[:, 0], mode_slopes, precision=highest)
    slope_imag = jnp.einsum("sqpj,zj->zsqp", coefficients[:, 1], mode_slopes, precision=highest)
    fields = (
        lax.all_to_all(value_real, "col", split_axis=0, concat_axis=3, tiled=True),
        lax.all_to_all(value_imag, "col", split_axis=0, concat_axis=3, tiled=True),
        lax.all_to_all(slope_real, "col", split_axis=0, concat_axis=3, tiled=True),
        lax.all_to_all(slope_imag, "col", split_axis=0, concat_axis=3, tiled=True),
    )
    fields = (
        lax.all_to_all(fields[0], "row", split_axis=2, concat_axis=3, tiled=True),
        lax.all_to_all(fields[1], "row", split_axis=2, concat_axis=3, tiled=True),
        lax.all_to_all(fields[2], "row", split_axis=2, concat_axis=3, tiled=True),
        lax.all_to_all(fields[3], "row", split_axis=2, concat_axis=3, tiled=True),
    )
    level_rows = fields[0].shape[0]
    span_rows = fields[0].shape[2]
    grid_shape = (level_rows, 2, span_rows, short_size, lane_width)
    value_real = fields[0].reshape(grid_shape)
    value_imag = fields[1].reshape(grid_shape)
    slope_real = fields[2].reshape(grid_shape)
    slope_imag = fields[3].reshape(grid_shape)
    wave_grid = zonal_waves.reshape(short_size, lane_width)
    scalar_real, scalar_imag = inverse_transform(value_real, value_imag, total_points)
    zonal_real, zonal_imag = inverse_transform(
        -wave_grid * value_imag, wave_grid * value_real, total_points
    )
    rise_real, rise_imag = inverse_transform(slope_real, slope_imag, total_points)
    flow = jnp.swapaxes(velocity.reshape(3, level_rows, lane_width, short_size), -1, -2)
    zonal_flow = flow[0][:, None, None]
    span_flow = flow[1][:, None, None]
    rise_flow = flow[2][:, None, None]
    span_waves = lax.dynamic_slice_in_dim(
        span_wavenumbers, lax.axis_index("row") * span_rows, span_rows
    )[None, None, :, None, None]
    background = jnp.transpose(gradient)[:, :, None, None, None]
    advect_real = (
        zonal_flow * zonal_real
        - span_waves * span_flow * scalar_imag
        + rise_flow * rise_real
        + rise_flow * background
    )
    advect_imag = (
        zonal_flow * zonal_imag + span_waves * span_flow * scalar_real + rise_flow * rise_imag
    )
    spectra_real, spectra_imag = forward_transform(advect_real, advect_imag, total_points)
    retained = (
        (jnp.abs(signed) <= total_points // 3).astype(jnp.float32).reshape(short_size, lane_width)
    )
    flat_shape = (level_rows, 2, span_rows, total_points)
    spectra_real = (spectra_real * retained).reshape(flat_shape)
    spectra_imag = (spectra_imag * retained).reshape(flat_shape)
    returned_real, returned_imag = (
        lax.all_to_all(
            lax.all_to_all(spectra_real, "row", split_axis=3, concat_axis=2, tiled=True),
            "col",
            split_axis=3,
            concat_axis=0,
            tiled=True,
        ),
        lax.all_to_all(
            lax.all_to_all(spectra_imag, "row", split_axis=3, concat_axis=2, tiled=True),
            "col",
            split_axis=3,
            concat_axis=0,
            tiled=True,
        ),
    )
    forcing_real = jnp.einsum("zsqp,jz->sqpj", returned_real, dual_modes, precision=highest)
    forcing_imag = jnp.einsum("zsqp,jz->sqpj", returned_imag, dual_modes, precision=highest)
    forcing = jnp.stack([forcing_real, forcing_imag], 1)
    denominator = 1.0 + implicit_rates[:, None, None, None, None] * (
        eigenvalues[None, None, None, None, :]
        + own_waves[None, None, None, :, None] ** 2
        + span_wavenumbers[None, None, :, None, None] ** 2
    )
    return (coefficients - time_step * forcing) / denominator


def solution(mesh):
    in_specs = (
        P(None, None, None, ("row", "col"), None),
        P(),
        P(),
        P(),
        P(),
        P(None, "col", None),
        P(None, "col"),
        P(),
        P(),
        P(),
    )
    out_specs = P(None, None, None, ("row", "col"), None)
    return jax.shard_map(
        on_device, mesh=mesh, in_specs=in_specs, out_specs=out_specs, check_vma=False
    )
```

profile of v0, /device:TPU:15, one launch (start us, length us, event | category | flops | bytes accessed | tf_op | source)
XLA Modules:
  0.0 696.5 jit_solution(4996307598044424374)
XLA Ops:
  36.5 33.1 %all-to-all-done.2 = f32[16,1,32768]{2,1,0:T(1,128)} async-done(((f32[16,1,32768]{2,1,0:T(1,128)}), f32[16,1,32768]{2,1,0:T(1,128)}, u32[]{:S(2)}, u32[]{:S(2)}) %all-to-all-start.2) | async-done | bytes 2097184 | tf_op jit(solution)/shard_map/all_to_all | solution.py:92
  89.6 33.0 %all-to-all-done = f32[16,1,32768]{2,1,0:T(1,128)} async-done(((f32[16,1,32768]{2,1,0:T(1,128)}), f32[16,1,32768]{2,1,0:T(1,128)}, u32[]{:S(2)}, u32[]{:S(2)}) %all-to-all-start) | async-done | bytes 2097184 | tf_op jit(solution)/shard_map/all_to_all | solution.py:93
  141.8 33.2 %all-to-all-done.4 = f32[16,1,32768]{2,1,0:T(1,128)} async-done(((f32[16,1,32768]{2,1,0:T(1,128)}), f32[16,1,32768]{2,1,0:T(1,128)}, u32[]{:S(2)}, u32[]{:S(2)}) %all-to-all-start.4) | async-done | bytes 2097184 | tf_op jit(solution)/shard_map/all_to_all | solution.py:94
  183.1 7.3 %reduce.2 = f32[16,32768]{1,0:T(8,128)S(1)} reduce(f32[16,1,32768]{2,1,0:T(1,128)} %all-to-all-done.2, f32[]{:T(128)} %broadcast.567), dimensions={1}, to_apply=%all_to_all.155.reduce_sub_computation | reduce | bytes 4194308 | tf_op jit(solution)/shard_map/all_to_all | solution.py:92
  193.4 6.6 copy.141
  205.2 22.4 %all-to-all-done.6 = f32[16,1,32768]{2,1,0:T(1,128)} async-done(((f32[16,1,32768]{2,1,0:T(1,128)}), f32[16,1,32768]{2,1,0:T(1,128)}, u32[]{:S(2)}, u32[]{:S(2)}) %all-to-all-start.6) | async-done | bytes 2097184 | tf_op jit(solution)/shard_map/all_to_all | solution.py:95
  239.4 7.3 %reduce.3 = f32[16,32768]{1,0:T(8,128)S(1)} reduce(f32[16,1,32768]{2,1,0:T(1,128)} %all-to-all-done, f32[]{:T(128)} %broadcast.567), dimensions={1}, to_apply=%all_to_all.148.reduce_sub_computation | reduce | bytes 4194308 | tf_op jit(solution)/shard_map/all_to_all | solution.py:93
  249.7 6.6 copy.140
  266.6 7.3 %reduce = f32[16,32768]{1,0:T(8,128)S(1)} reduce(f32[16,1,32768]{2,1,0:T(1,128)} %all-to-all-done.4, f32[]{:T(128)} %broadcast.567), dimensions={1}, to_apply=%all_to_all.162.reduce_sub_computation | reduce | bytes 4194308 | tf_op jit(solution)/shard_map/all_to_all | solution.py:94
  288.7 7.3 %reduce.1 = f32[16,32768]{1,0:T(8,128)S(1)} reduce(f32[16,1,32768]{2,1,0:T(1,128)} %all-to-all-done.6, f32[]{:T(128)} %broadcast.567), dimensions={1}, to_apply=%all_to_all.169.reduce_sub_computation | reduce | bytes 4194308 | tf_op jit(solution)/shard_map/all_to_all | solution.py:95
  299.3 6.6 copy.143
  351.1 6.7 all-to-all-done.5
  452.6 8.8 %reshape.206 = f32[2,1,262144]{2,1,0:T(1,128)} reshape(f32[2048,2,4,32]{3,2,1,0:T(4,128)} %bitcast.251) | data formatting | bytes 4194304
  479.9 8.8 %reshape.202 = f32[2,1,262144]{2,1,0:T(1,128)} reshape(f32[2048,2,4,32]{3,2,1,0:T(4,128)} %bitcast.252) | data formatting | bytes 4194304
  495.0 8.1 %reduce.6 = f32[2,262144]{1,0:T(2,128)S(1)} reduce(f32[2,1,262144]{2,1,0:T(1,128)} %all-to-all-done.8, f32[]{:T(128)} %broadcast.567), dimensions={1}, to_apply=%all_to_all.176.reduce_sub_computation | reduce | bytes 4194308 | tf_op jit(solution)/shard_map/all_to_all | solution.py:142
  503.1 8.2 %reshape.207 = f32[2048,2,4,32]{3,2,1,0:T(4,128)} reshape(f32[2,262144]{1,0:T(2,128)S(1)} %reduce.6) | data formatting | bytes 4194304
  511.4 6.9 copy.145
  520.2 7.5 %copy.116 = f32[32,2,8,1024]{0,2,1,3:T(8,128)} copy(f32[32,2,8,1024]{3,0,2,1:T(8,128)} %bitcast.267) | data formatting | bytes 4194304 | tf_op jit(solution)/shard_map/all_to_all | solution.py:142
  527.7 8.6 %reshape.208 = f32[16,1,32768]{2,1,0:T(1,128)} reshape(f32[1024,2,8,32]{3,2,1,0:T(8,128)} %bitcast.254) | data formatting | bytes 4194304
  536.3 7.7 %all-to-all-start.9 = ((f32[16,1,32768]{2,1,0:T(1,128)}), f32[16,1,32768]{2,1,0:T(1,128)}, u32[]{:S(2)}, u32[]{:S(2)}) async-start(f32[16,1,32768]{2,1,0:T(1,128)} %reshape.208), calls=%async_computation.9 | async-start | bytes 4194304 | tf_op jit(solution)/shard_map/all_to_all | solution.py:141
  544.0 8.1 %reduce.4 = f32[2,262144]{1,0:T(2,128)S(1)} reduce(f32[2,1,262144]{2,1,0:T(1,128)} %all-to-all-done.10, f32[]{:T(128)} %broadcast.567), dimensions={1}, to_apply=%all_to_all.184.reduce_sub_computation | reduce | bytes 4194308 | tf_op jit(solution)/shard_map/all_to_all | solution.py:149
  552.2 8.2 %reshape.203 = f32[2048,2,4,32]{3,2,1,0:T(4,128)} reshape(f32[2,262144]{1,0:T(2,128)S(1)} %reduce.4) | data formatting | bytes 4194304
  560.4 6.9 copy.149
  569.2 7.5 %copy.123 = f32[32,2,8,1024]{0,2,1,3:T(8,128)} copy(f32[32,2,8,1024]{3,0,2,1:T(8,128)} %bitcast.269) | data formatting | bytes 4194304 | tf_op jit(solution)/shard_map/all_to_all | solution.py:149
  576.7 8.6 %reshape.204 = f32[16,1,32768]{2,1,0:T(1,128)} reshape(f32[1024,2,8,32]{3,2,1,0:T(8,128)} %bitcast.256) | data formatting | bytes 4194304
  599.6 7.3 %reduce.7 = f32[16,32768]{1,0:T(8,128)S(1)} reduce(f32[16,1,32768]{2,1,0:T(1,128)} %all-to-all-done.9, f32[]{:T(128)} %broadcast.567), dimensions={1}, to_apply=%all_to_all.180.reduce_sub_computation | reduce | bytes 4194308 | tf_op jit(solution)/shard_map/all_to_all | solution.py:141
  611.7 7.0 copy.156
  618.7 25.6 %all-to-all-done.11 = f32[16,1,32768]{2,1,0:T(1,128)} async-done(((f32[16,1,32768]{2,1,0:T(1,128)}), f32[16,1,32768]{2,1,0:T(1,128)}, u32[]{:S(2)}, u32[]{:S(2)}) %all-to-all-start.11) | async-done | bytes 2097184 | tf_op jit(solution)/shard_map/all_to_all | solution.py:148
  644.3 7.3 %reduce.5 = f32[16,32768]{1,0:T(8,128)S(1)} reduce(f32[16,1,32768]{2,1,0:T(1,128)} %all-to-all-done.11, f32[]{:T(128)} %broadcast.567), dimensions={1}, to_apply=%all_to_all.188.reduce_sub_computation | reduce | bytes 4194308 | tf_op jit(solution)/shard_map/all_to_all | solution.py:148
  656.4 6.9 copy.157
  663.3 15.3 %convolution_bitcast_fusion.1 = f32[2,1,8,64,512]{4,3,2,0,1:T(8,128)S(1)} fusion(f32[512,2,8,64]{3,0,2,1:T(8,128)} %bitcast.259, f32[512,512]{1,0:T(8,128)S(1)} %copy-done.20), kind=kOutput, calls=%fused_computation.57 | convolution fusion | flops 3221225472 | bytes 5242880 | tf_op jit(solution)/shard_map/zsqp,jz->sqpj/dot_general | solution.py:156
  678.7 13.3 %convolution_bitcast_fusion = f32[2,1,8,64,512]{4,3,2,0,1:T(8,128)S(1)} fusion(f32[512,2,8,64]{3,0,2,1:T(8,128)S(1)} %bitcast.260, f32[512,512]{1,0:T(8,128)S(1)} %copy-done.20), kind=kOutput, calls=%fused_computation.56 | convolution fusion | flops 3221225472 | bytes 5242880 | tf_op jit(solution)/shard_map/zsqp,jz->sqpj/dot_general | solution.py:157
  (168 shorter events, 330.6 us)
Async XLA Ops:
  15.6 54.1 %all-to-all-start.2 = ((f32[16,1,32768]{2,1,0:T(1,128)}), f32[16,1,32768]{2,1,0:T(1,128)}, u32[]{:S(2)}, u32[]{:S(2)}) async-start(f32[16,1,32768]{2,1,0:T(1,128)} %reshape.198), calls=%async_computation.2 | async-start | bytes 4194304 | tf_op jit(solution)/shard_map/all_to_all | solution.py:92
  36.5 38.7 %copy-start.19 = (f32[512,512]{1,0:T(8,128)S(1)}, f32[512,512]{1,0:T(8,128)}, u32[]{:S(2)}) copy-start(f32[512,512]{1,0:T(8,128)} %param.12) | copy-start | bytes 3145732
  69.7 52.9 %all-to-all-start = ((f32[16,1,32768]{2,1,0:T(1,128)}), f32[16,1,32768]{2,1,0:T(1,128)}, u32[]{:S(2)}, u32[]{:S(2)}) async-start(f32[16,1,32768]{2,1,0:T(1,128)} %reshape.200), calls=%async_computation | async-start | bytes 4194304 | tf_op jit(solution)/shard_map/all_to_all | solution.py:93
  122.5 52.4 %all-to-all-start.4 = ((f32[16,1,32768]{2,1,0:T(1,128)}), f32[16,1,32768]{2,1,0:T(1,128)}, u32[]{:S(2)}, u32[]{:S(2)}) async-start(f32[16,1,32768]{2,1,0:T(1,128)} %reshape.194), calls=%async_computation.4 | async-start | bytes 4194304 | tf_op jit(solution)/shard_map/all_to_all | solution.py:94
  141.8 38.4 %copy-start.24 = (f32[3,32,2048]{2,1,0:T(8,128)S(1)}, f32[3,32,2048]{2,1,0:T(8,128)}, u32[]{:S(2)}) copy-start(f32[3,32,2048]{2,1,0:T(8,128)} %param.15) | copy-start | bytes 2359300
  175.0 52.6 %all-to-all-start.6 = ((f32[16,1,32768]{2,1,0:T(1,128)}), f32[16,1,32768]{2,1,0:T(1,128)}, u32[]{:S(2)}, u32[]{:S(2)}) async-start(f32[16,1,32768]{2,1,0:T(1,128)} %reshape.196), calls=%async_computation.6 | async-start | bytes 4194304 | tf_op jit(solution)/shard_map/all_to_all | solution.py:95
  227.6 34.0 %all-to-all-start.3 = ((f32[32,2,8,1024]{3,1,0,2:T(2,128)}), f32[32,2,8,1024]{3,1,0,2:T(2,128)}, u32[]{:S(2)}, u32[]{:S(2)}) async-start(f32[32,2,8,1024]{3,1,0,2:T(2,128)} %reshape.191), calls=%async_computation.3 | async-start | bytes 4194304 | tf_op jit(solution)/shard_map/all_to_all | solution.py:98
  235.1 2.9 copy-start.26
  235.1 2.9 copy-start.28
  236.3 2.9 copy-start.23
  261.5 67.8 %all-to-all-start.1 = ((f32[32,2,8,1024]{3,1,0,2:T(2,128)}), f32[32,2,8,1024]{3,1,0,2:T(2,128)}, u32[]{:S(2)}, u32[]{:S(2)}) async-start(f32[32,2,8,1024]{3,1,0,2:T(2,128)} %reshape.190), calls=%async_computation.1 | async-start | bytes 4194304 | tf_op jit(solution)/shard_map/all_to_all | solution.py:99
  329.3 28.5 %all-to-all-start.5 = ((f32[32,2,8,1024]{3,1,0,2:T(2,128)}), f32[32,2,8,1024]{3,1,0,2:T(2,128)}, u32[]{:S(2)}, u32[]{:S(2)}) async-start(f32[32,2,8,1024]{3,1,0,2:T(2,128)} %reshape.192), calls=%async_computation.5 | async-start | bytes 4194304 | tf_op jit(solution)/shard_map/all_to_all | solution.py:100
  343.5 2.2 copy-start.12
  357.9 30.3 %all-to-all-start.7 = ((f32[32,2,8,1024]{3,1,0,2:T(2,128)}), f32[32,2,8,1024]{3,1,0,2:T(2,128)}, u32[]{:S(2)}, u32[]{:S(2)}) async-start(f32[32,2,8,1024]{3,1,0,2:T(2,128)} %reshape.193), calls=%async_computation.7 | async-start | bytes 4194304 | tf_op jit(solution)/shard_map/all_to_all | solution.py:101
  373.1 5.0 copy-start.10
  378.1 3.2 copy-start.3
  397.8 4.4 copy-start.9
  397.8 4.4 copy-start.13
  423.6 2.4 copy-start.21
  423.6 2.4 copy-start.22
  461.4 27.3 %all-to-all-start.8 = ((f32[2,1,262144]{2,1,0:T(1,128)}), f32[2,1,262144]{2,1,0:T(1,128)}, u32[]{:S(2)}, u32[]{:S(2)}) async-start(f32[2,1,262144]{2,1,0:T(1,128)} %reshape.206), calls=%async_computation.8 | async-start | bytes 4194304 | tf_op jit(solution)/shard_map/all_to_all | solution.py:142
  466.4 3.7 copy-start.6
  488.7 47.5 %all-to-all-start.10 = ((f32[2,1,262144]{2,1,0:T(1,128)}), f32[2,1,262144]{2,1,0:T(1,128)}, u32[]{:S(2)}, u32[]{:S(2)}) async-start(f32[2,1,262144]{2,1,0:T(1,128)} %reshape.202), calls=%async_computation.10 | async-start | bytes 4194304 | tf_op jit(solution)/shard_map/all_to_all | solution.py:149
  536.3 55.1 %all-to-all-start.9 = ((f32[16,1,32768]{2,1,0:T(1,128)}), f32[16,1,32768]{2,1,0:T(1,128)}, u32[]{:S(2)}, u32[]{:S(2)}) async-start(f32[16,1,32768]{2,1,0:T(1,128)} %reshape.208), calls=%async_computation.9 | async-start | bytes 4194304 | tf_op jit(solution)/shard_map/all_to_all | solution.py:141
  585.3 12.3 %copy-start.25 = (f32[512]{0:T(512)S(1)}, f32[512]{0:T(512)}, u32[]{:S(2)}) copy-start(f32[512]{0:T(512)} %param.14) | copy-start | bytes 6148
  585.3 12.6 %copy-start.27 = (f32[2]{0:T(128)S(1)}, f32[2]{0:T(128)}, u32[]{:S(2)}) copy-start(f32[2]{0:T(128)} %param.18) | copy-start | bytes 28
  591.4 52.9 %all-to-all-start.11 = ((f32[16,1,32768]{2,1,0:T(1,128)}), f32[16,1,32768]{2,1,0:T(1,128)}, u32[]{:S(2)}, u32[]{:S(2)}) async-start(f32[16,1,32768]{2,1,0:T(1,128)} %reshape.204), calls=%async_computation.11 | async-start | bytes 4194304 | tf_op jit(solution)/shard_map/all_to_all | solution.py:148
  656.4 6.9 copy-start.20
  663.3 15.4 %copy-start.11 = (f32[16,32,2,8,64]{4,1,0,3,2:T(8,128)S(1)}, f32[16,32,2,8,64]{4,1,0,3,2:T(8,128)}, u32[]{:S(2)}) copy-start(f32[16,32,2,8,64]{4,1,0,3,2:T(8,128)} %copy.157) | copy-start | bytes 6291460
  678.7 13.4 %copy-start.2 = (f32[2,2,8,64,512]{4,3,2,1,0:T(8,128)S(1)}, f32[2,2,8,64,512]{4,3,2,1,0:T(8,128)}, u32[]{:S(2)}) copy-start(f32[2,2,8,64,512]{4,3,2,1,0:T(8,128)} %param.10) | copy-start | bytes 12582916
  678.7 13.4 %copy-start.16 = (f32[2,8,64,512]{3,2,1,0:T(8,128)S(1)}, f32[2,8,64,512]{3,2,1,0:T(8,128)}, u32[]{:S(2)}) copy-start(f32[2,8,64,512]{3,2,1,0:T(8,128)} %multiply_add_fusion) | copy-start | bytes 6291460
  693.7 2.6 copy-start.1
  (9 other events, 18.1 us)
where the time goes:
time: 707 us; the launch traced here: 696 us
  local copies, waits for them, and re-layouts  266 us (38%)
  waiting for transfers between devices  160 us (23%)
  matrix products  136 us (19%)
  starting transfers between devices  67.9 us (10%)
  other arithmetic  65.1 us (9%)
    unnamed x75, local copies, waits for them, and re-layouts  99.1 us
    all_to_all x1, waiting for transfers between devices, on_device(): lax.all_to_all(slope_real, 'col', split_axis=0, concat_axis=3, tiled=True)  33.2 us
    all_to_all x1, waiting for transfers between devices, on_device(): lax.all_to_all(value_real, 'col', split_axis=0, concat_axis=3, tiled=True)  33.1 us
    all_to_all x1, waiting for transfers between devices, on_device(): lax.all_to_all(value_imag, 'col', split_axis=0, concat_axis=3, tiled=True)  33 us
    all_to_all x1, waiting for transfers between devices, on_device(): lax.all_to_all(lax.all_to_all(spectra_imag, 'row', split_axis=3, concat_a...  25.6 us
    dot_general x8, matrix products, contract(): jnp.einsum(form, left_imag, right_imag, precision=highest)  24.6 us
    all_to_all x1, waiting for transfers between devices, on_device(): lax.all_to_all(slope_imag, 'col', split_axis=0, concat_axis=3, tiled=True)  22.4 us
    dot_general x8, matrix products, contract(): jnp.einsum(form, left_real, right_real, precision=highest)  21.7 us
  transfers between devices with their start and end apart: 12, of which 7 were waited for; matrix products, arithmetic and copies ran while one was open for 47% of the time, Pallas kernels for 0%

commit v1 on v0

--- a/solution.py
+++ b/solution.py
@@ -6,6 +6,22 @@
 
 highest = lax.Precision.HIGHEST
 lane_width = 128
+
+
+def exchange_in_pairs(x, axis, split, join):
+    ways, here = (lax.axis_size(axis), lax.axis_index(axis))
+    width = x.shape[split] // ways
+    lengths = list(x.shape)
+    lengths[split] = width
+    height = lengths[join]
+    lengths[join] = height * ways
+    full = jnp.zeros(lengths, x.dtype)
+    for mask in range(ways):
+        part = lax.dynamic_slice_in_dim(x, (here ^ mask) * width, width, axis=split)
+        if mask:
+            part = lax.ppermute(part, axis, [(d, d ^ mask) for d in range(ways)])
+        full = lax.dynamic_update_slice_in_dim(full, part, (here ^ mask) * height, axis=join)
+    return full
 
 
 def signed_waves(length):
@@ -90,7 +106,7 @@
     slope_imag = jnp.einsum("sqpj,zj->zsqp", coefficients[:, 1], mode_slopes, precision=highest)
     fields = (
         lax.all_to_all(value_real, "col", split_axis=0, concat_axis=3, tiled=True),
-        lax.all_to_all(value_imag, "col", split_axis=0, concat_axis=3, tiled=True),
+        exchange_in_pairs(value_imag, "col", 0, 3),
         lax.all_to_all(slope_real, "col", split_axis=0, concat_axis=3, tiled=True),
         lax.all_to_all(slope_imag, "col", split_axis=0, concat_axis=3, tiled=True),
     )

time: 707 us -> 843 us (1.19)
  waiting for transfers between devices: 160 us -> 251 us
  local copies, waits for them, and re-layouts: 266 us -> 304 us
  starting transfers between devices: 67.9 us -> 84.2 us
    ppermute x0 -> x15, waiting for transfers between devices: none -> 130 us  [exchange_in_pairs(): part = lax.ppermute(part, axis, [(d, d ^ mask) for d in range(ways)])]
    dynamic_update_slice x0 -> x16, local copies, waits for them, and re-layouts: none -> 47.9 us  [exchange_in_pairs(): lax.dynamic_update_slice_in_dim(full, part, (here ^ mask) * height, axis=...]
    all_to_all x1 -> x0, waiting for transfers between devices: 33 us -> none  [on_device(): lax.all_to_all(value_imag, 'col', split_axis=0, concat_axis=3, tiled=True)]
    ppermute x0 -> x15, starting transfers between devices: none -> 17.6 us  [exchange_in_pairs(): part = lax.ppermute(part, axis, [(d, d ^ mask) for d in range(ways)])]
    all_to_all x2 -> x0, local copies, waits for them, and re-layouts: 11.8 us -> none  [on_device(): lax.all_to_all(value_imag, 'col', split_axis=0, concat_axis=3, tiled=True)]
    ppermute x0 -> x15, local copies, waits for them, and re-layouts: none -> 10.1 us  [exchange_in_pairs(): part = lax.ppermute(part, axis, [(d, d ^ mask) for d in range(ways)])]
    unnamed x75 -> x97, local copies, waits for them, and re-layouts: 99.1 us -> 92.6 us
  transfers between devices with their start and end apart: 12 -> 26, of which waited for: 7 -> 14; matrix products, arithmetic and copies ran while one was open for 47% -> 43% of each run, Pallas kernels for 0% -> 0%
where the time goes in v1:
time: 843 us; the launch traced here: 833 us
  local copies, waits for them, and re-layouts  304 us (36%)
  waiting for transfers between devices  251 us (30%)
  matrix products  135 us (16%)
  starting transfers between devices  84.2 us (10%)
  other arithmetic  57.3 us (7%)
    ppermute x15, waiting for transfers between devices, exchange_in_pairs(): part = lax.ppermute(part, axis, [(d, d ^ mask) for d in range(ways)])  130 us
    unnamed x97, local copies, waits for them, and re-layouts  92.6 us
    dynamic_update_slice x16, local copies, waits for them, and re-layouts, exchange_in_pairs(): lax.dynamic_update_slice_in_dim(full, part, (here ^ mask) * height, axis=...  47.9 us
    all_to_all x1, waiting for transfers between devices, on_device(): lax.all_to_all(slope_real, 'col', split_axis=0, concat_axis=3, tiled=True)  33.1 us
    all_to_all x1, waiting for transfers between devices, on_device(): lax.all_to_all(value_real, 'col', split_axis=0, concat_axis=3, tiled=True)  33.1 us
    all_to_all x1, waiting for transfers between devices, on_device(): lax.all_to_all(lax.all_to_all(spectra_imag, 'row', split_axis=3, concat_a...  25.4 us
    dot_general x8, matrix products, contract(): jnp.einsum(form, left_imag, right_imag, precision=highest)  23 us
    dot_general x8, matrix products, contract(): jnp.einsum(form, left_real, right_real, precision=highest)  21.9 us
  transfers between devices with their start and end apart: 26, of which 14 were waited for; matrix products, arithmetic and copies ran while one was open for 43% of the time, Pallas kernels for 0%

profile of v1, /device:TPU:15, one launch (start us, length us, event | category | flops | bytes accessed | tf_op | source)
XLA Modules:
  0.0 833.4 jit_solution(10487942545330814953)
XLA Ops:
  15.2 9.1 %collective-permute-done.1 = f32[32,2,8,64]{0,3,2,1:T(8,128)S(1)} collective-permute-done((f32[32,2,8,64]{0,3,2,1:T(8,128)S(1)}, f32[32,2,8,64]{0,3,2,1:T(8,128)S(1)}, u32[]{:S(2)}, u32[]{:S(2)}) %collective-permute-start.1) | collective-permute-done | bytes 131104 | tf_op jit(solution)/shard_map/ppermute | solution.py:22
  26.3 9.6 %collective-permute-done.2 = f32[32,2,8,64]{0,3,2,1:T(8,128)S(1)} collective-permute-done((f32[32,2,8,64]{0,3,2,1:T(8,128)S(1)}, f32[32,2,8,64]{0,3,2,1:T(8,128)S(1)}, u32[]{:S(2)}, u32[]{:S(2)}) %collective-permute-start.2) | collective-permute-done | bytes 131104 | tf_op jit(solution)/shard_map/ppermute | solution.py:22
  40.8 27.9 %collective-permute-done.5 = f32[32,2,8,64]{0,3,2,1:T(8,128)S(1)} collective-permute-done((f32[32,2,8,64]{0,3,2,1:T(8,128)S(1)}, f32[32,2,8,64]{0,3,2,1:T(8,128)S(1)}, u32[]{:S(2)}, u32[]{:S(2)}) %collective-permute-start.5) | collective-permute-done | bytes 131104 | tf_op jit(solution)/shard_map/ppermute | solution.py:22
  82.6 45.7 %collective-permute-done.8 = f32[32,2,8,64]{0,3,2,1:T(8,128)S(1)} collective-permute-done((f32[32,2,8,64]{0,3,2,1:T(8,128)S(1)}, f32[32,2,8,64]{0,3,2,1:T(8,128)S(1)}, u32[]{:S(2)}, u32[]{:S(2)}) %collective-permute-start.8) | collective-permute-done | bytes 131104 | tf_op jit(solution)/shard_map/ppermute | solution.py:22
  128.3 22.5 %collective-permute-done.9 = f32[32,2,8,64]{0,3,2,1:T(8,128)S(1)} collective-permute-done((f32[32,2,8,64]{0,3,2,1:T(8,128)S(1)}, f32[32,2,8,64]{0,3,2,1:T(8,128)S(1)}, u32[]{:S(2)}, u32[]{:S(2)}) %collective-permute-start.9) | collective-permute-done | bytes 131104 | tf_op jit(solution)/shard_map/ppermute | solution.py:22
  246.1 9.5 %all-to-all-start.1 = ((f32[16,1,32768]{2,1,0:T(1,128)}), f32[16,1,32768]{2,1,0:T(1,128)}, u32[]{:S(2)}, u32[]{:S(2)}) async-start(f32[16,1,32768]{2,1,0:T(1,128)} %reshape.197), calls=%async_computation.1 | async-start | bytes 4194304 | tf_op jit(solution)/shard_map/all_to_all | solution.py:108
  270.0 33.1 %all-to-all-done.1 = f32[16,1,32768]{2,1,0:T(1,128)} async-done(((f32[16,1,32768]{2,1,0:T(1,128)}), f32[16,1,32768]{2,1,0:T(1,128)}, u32[]{:S(2)}, u32[]{:S(2)}) %all-to-all-start.1) | async-done | bytes 2097184 | tf_op jit(solution)/shard_map/all_to_all | solution.py:108
  322.4 33.1 %all-to-all-done.3 = f32[16,1,32768]{2,1,0:T(1,128)} async-done(((f32[16,1,32768]{2,1,0:T(1,128)}), f32[16,1,32768]{2,1,0:T(1,128)}, u32[]{:S(2)}, u32[]{:S(2)}) %all-to-all-start.3) | async-done | bytes 2097184 | tf_op jit(solution)/shard_map/all_to_all | solution.py:110
  368.9 7.3 reduce.2
  391.1 17.3 %all-to-all-done.5 = f32[16,1,32768]{2,1,0:T(1,128)} async-done(((f32[16,1,32768]{2,1,0:T(1,128)}), f32[16,1,32768]{2,1,0:T(1,128)}, u32[]{:S(2)}, u32[]{:S(2)}) %all-to-all-start.5) | async-done | bytes 2097184 | tf_op jit(solution)/shard_map/all_to_all | solution.py:111
  422.0 7.3 reduce
  444.5 7.3 reduce.1
  589.8 8.8 %reshape.203 = f32[2,1,262144]{2,1,0:T(1,128)} reshape(f32[2048,2,4,32]{3,2,1,0:T(4,128)} %bitcast.244) | data formatting | bytes 4194304
  617.2 8.8 %reshape.199 = f32[2,1,262144]{2,1,0:T(1,128)} reshape(f32[2048,2,4,32]{3,2,1,0:T(4,128)} %bitcast.245) | data formatting | bytes 4194304
  632.3 8.1 reduce.5
  640.4 8.3 reshape.204
  648.7 6.9 copy.184
  657.6 7.5 copy.155
  665.1 8.6 %reshape.205 = f32[16,1,32768]{2,1,0:T(1,128)} reshape(f32[1024,2,8,32]{3,2,1,0:T(8,128)} %bitcast.247) | data formatting | bytes 4194304
  673.6 7.7 all-to-all-start.8
  681.4 8.1 reduce.3
  689.5 8.3 reshape.200
  697.7 6.9 copy.188
  706.5 7.5 copy.162
  714.0 8.6 %reshape.201 = f32[16,1,32768]{2,1,0:T(1,128)} reshape(f32[1024,2,8,32]{3,2,1,0:T(8,128)} %bitcast.249) | data formatting | bytes 4194304
  736.6 7.3 reduce.6
  748.7 7.3 copy.194
  756.0 25.4 %all-to-all-done.10 = f32[16,1,32768]{2,1,0:T(1,128)} async-done(((f32[16,1,32768]{2,1,0:T(1,128)}), f32[16,1,32768]{2,1,0:T(1,128)}, u32[]{:S(2)}, u32[]{:S(2)}) %all-to-all-start.10) | async-done | bytes 2097184 | tf_op jit(solution)/shard_map/all_to_all | solution.py:164
  781.4 7.3 reduce.4
  793.4 6.9 copy.195
  800.3 15.3 %convolution_bitcast_fusion.1 = f32[2,1,8,64,512]{4,3,2,0,1:T(8,128)S(1)} fusion(f32[512,2,8,64]{3,0,2,1:T(8,128)} %bitcast.252, f32[512,512]{1,0:T(8,128)S(1)} %copy-done.19), kind=kOutput, calls=%fused_computation.57 | convolution fusion | flops 3221225472 | bytes 5242880 | tf_op jit(solution)/shard_map/zsqp,jz->sqpj/dot_general | solution.py:172
  815.7 13.3 %convolution_bitcast_fusion = f32[2,1,8,64,512]{4,3,2,0,1:T(8,128)S(1)} fusion(f32[512,2,8,64]{3,0,2,1:T(8,128)S(1)} %bitcast.253, f32[512,512]{1,0:T(8,128)S(1)} %copy-done.19), kind=kOutput, calls=%fused_computation.56 | convolution fusion | flops 3221225472 | bytes 5242880 | tf_op jit(solution)/shard_map/zsqp,jz->sqpj/dot_general | solution.py:173
  (247 shorter events, 415.3 us)
Async XLA Ops:
  10.1 4.2 collective-permute-start
  10.8 13.6 %collective-permute-start.1 = (f32[32,2,8,64]{0,3,2,1:T(8,128)S(1)}, f32[32,2,8,64]{0,3,2,1:T(8,128)S(1)}, u32[]{:S(2)}, u32[]{:S(2)}) collective-permute-start(f32[32,2,8,64]{0,3,2,1:T(8,128)S(1)} %get-tuple-element.21), channel_id=1, source_target_pairs={{0,2},{1,3},{2,0},{3,1},{4,6},{5,7},{6,4},{7,5},{8,10},{9,11},{10,... | collective-permute-start | bytes 393224 | tf_op jit(solution)/shard_map/ppermute | solution.py:22
  11.0 24.9 %collective-permute-start.2 = (f32[32,2,8,64]{0,3,2,1:T(8,128)S(1)}, f32[32,2,8,64]{0,3,2,1:T(8,128)S(1)}, u32[]{:S(2)}, u32[]{:S(2)}) collective-permute-start(f32[32,2,8,64]{0,3,2,1:T(8,128)S(1)} %get-tuple-element.20), channel_id=1, source_target_pairs={{0,3},{1,2},{2,1},{3,0},{4,7},{5,6},{6,5},{7,4},{8,11},{9,10},{10,... | collective-permute-start | bytes 393224 | tf_op jit(solution)/shard_map/ppermute | solution.py:22
  12.4 25.9 %collective-permute-start.3 = (f32[32,2,8,64]{0,3,2,1:T(8,128)S(1)}, f32[32,2,8,64]{0,3,2,1:T(8,128)S(1)}, u32[]{:S(2)}, u32[]{:S(2)}) collective-permute-start(f32[32,2,8,64]{0,3,2,1:T(8,128)S(1)} %get-tuple-element.19), channel_id=1, source_target_pairs={{0,4},{1,5},{2,6},{3,7},{4,0},{5,1},{6,2},{7,3},{8,12},{9,13},{10,... | collective-permute-start | bytes 393224 | tf_op jit(solution)/shard_map/ppermute | solution.py:22
  12.6 25.9 %collective-permute-start.4 = (f32[32,2,8,64]{0,3,2,1:T(8,128)S(1)}, f32[32,2,8,64]{0,3,2,1:T(8,128)S(1)}, u32[]{:S(2)}, u32[]{:S(2)}) collective-permute-start(f32[32,2,8,64]{0,3,2,1:T(8,128)S(1)} %get-tuple-element.18), channel_id=1, source_target_pairs={{0,5},{1,4},{2,7},{3,6},{4,1},{5,0},{6,3},{7,2},{8,13},{9,12},{10,... | collective-permute-start | bytes 393224 | tf_op jit(solution)/shard_map/ppermute | solution.py:22
  15.1 53.6 %collective-permute-start.5 = (f32[32,2,8,64]{0,3,2,1:T(8,128)S(1)}, f32[32,2,8,64]{0,3,2,1:T(8,128)S(1)}, u32[]{:S(2)}, u32[]{:S(2)}) collective-permute-start(f32[32,2,8,64]{0,3,2,1:T(8,128)S(1)} %get-tuple-element.17), channel_id=1, source_target_pairs={{0,6},{1,7},{2,4},{3,5},{4,2},{5,3},{6,0},{7,1},{8,14},{9,15},{10,... | collective-permute-start | bytes 393224 | tf_op jit(solution)/shard_map/ppermute | solution.py:22
  25.1 54.8 %collective-permute-start.6 = (f32[32,2,8,64]{0,3,2,1:T(8,128)S(1)}, f32[32,2,8,64]{0,3,2,1:T(8,128)S(1)}, u32[]{:S(2)}, u32[]{:S(2)}) collective-permute-start(f32[32,2,8,64]{0,3,2,1:T(8,128)S(1)} %get-tuple-element.16), channel_id=1, source_target_pairs={{0,7},{1,6},{2,5},{3,4},{4,3},{5,2},{6,1},{7,0},{8,15},{9,14},{10,... | collective-permute-start | bytes 393224 | tf_op jit(solution)/shard_map/ppermute | solution.py:22
  35.9 114.8 %copy-start.26 = (f32[32,2,8,64]{0,3,2,1:T(8,128)}, f32[32,2,8,64]{0,3,2,1:T(8,128)S(1)}, u32[]{:S(2)}) copy-start(f32[32,2,8,64]{0,3,2,1:T(8,128)S(1)} %collective-permute-done.2) | copy-start | bytes 393220
  35.9 44.2 %collective-permute-start.7 = (f32[32,2,8,64]{0,3,2,1:T(8,128)S(1)}, f32[32,2,8,64]{0,3,2,1:T(8,128)S(1)}, u32[]{:S(2)}, u32[]{:S(2)}) collective-permute-start(f32[32,2,8,64]{0,3,2,1:T(8,128)S(1)} %get-tuple-element.15), channel_id=1, source_target_pairs={{0,8},{1,9},{2,10},{3,11},{4,12},{5,13},{6,14},{7,15},{8,0},{9,1},... | collective-permute-start | bytes 393224 | tf_op jit(solution)/shard_map/ppermute | solution.py:22
  38.3 90.0 %collective-permute-start.8 = (f32[32,2,8,64]{0,3,2,1:T(8,128)S(1)}, f32[32,2,8,64]{0,3,2,1:T(8,128)S(1)}, u32[]{:S(2)}, u32[]{:S(2)}) collective-permute-start(f32[32,2,8,64]{0,3,2,1:T(8,128)S(1)} %get-tuple-element.14), channel_id=1, source_target_pairs={{0,9},{1,8},{2,11},{3,10},{4,13},{5,12},{6,15},{7,14},{8,1},{9,0},... | collective-permute-start | bytes 393224 | tf_op jit(solution)/shard_map/ppermute | solution.py:22
  38.5 112.3 %collective-permute-start.9 = (f32[32,2,8,64]{0,3,2,1:T(8,128)S(1)}, f32[32,2,8,64]{0,3,2,1:T(8,128)S(1)}, u32[]{:S(2)}, u32[]{:S(2)}) collective-permute-start(f32[32,2,8,64]{0,3,2,1:T(8,128)S(1)} %get-tuple-element.13), channel_id=1, source_target_pairs={{0,10},{1,11},{2,8},{3,9},{4,14},{5,15},{6,12},{7,13},{8,2},{9,3},... | collective-permute-start | bytes 393224 | tf_op jit(solution)/shard_map/ppermute | solution.py:22
  68.7 82.1 %copy-start.24 = (f32[32,2,8,64]{0,3,2,1:T(8,128)}, f32[32,2,8,64]{0,3,2,1:T(8,128)S(1)}, u32[]{:S(2)}) copy-start(f32[32,2,8,64]{0,3,2,1:T(8,128)S(1)} %collective-permute-done.5) | copy-start | bytes 393220
  68.7 123.9 %collective-permute-start.10 = (f32[32,2,8,64]{0,3,2,1:T(8,128)}, f32[32,2,8,64]{0,3,2,1:T(8,128)}, u32[]{:S(2)}, u32[]{:S(2)}) collective-permute-start(f32[32,2,8,64]{0,3,2,1:T(8,128)} %get-tuple-element.12), channel_id=1, source_target_pairs={{0,11},{1,10},{2,9},{3,8},{4,15},{5,14},{6,13},{7,12},{8,3},{9,2},... | collective-permute-start | bytes 393224 | tf_op jit(solution)/shard_map/ppermute | solution.py:22
  80.0 70.8 %copy-start.27 = (f32[32,2,8,64]{0,3,2,1:T(8,128)}, f32[32,2,8,64]{0,3,2,1:T(8,128)S(1)}, u32[]{:S(2)}) copy-start(f32[32,2,8,64]{0,3,2,1:T(8,128)S(1)} %collective-permute-done.6) | copy-start | bytes 393220
  80.0 115.8 %collective-permute-start.11 = (f32[32,2,8,64]{0,3,2,1:T(8,128)}, f32[32,2,8,64]{0,3,2,1:T(8,128)}, u32[]{:S(2)}, u32[]{:S(2)}) collective-permute-start(f32[32,2,8,64]{0,3,2,1:T(8,128)} %get-tuple-element.11), channel_id=1, source_target_pairs={{0,12},{1,13},{2,14},{3,15},{4,8},{5,9},{6,10},{7,11},{8,4},{9,5},... | collective-permute-start | bytes 393224 | tf_op jit(solution)/shard_map/ppermute | solution.py:22
  80.1 70.7 %copy-start.30 = (f32[32,2,8,64]{0,3,2,1:T(8,128)}, f32[32,2,8,64]{0,3,2,1:T(8,128)S(1)}, u32[]{:S(2)}) copy-start(f32[32,2,8,64]{0,3,2,1:T(8,128)S(1)} %collective-permute-done.7) | copy-start | bytes 393220
  80.1 121.0 %collective-permute-start.12 = (f32[32,2,8,64]{0,3,2,1:T(8,128)}, f32[32,2,8,64]{0,3,2,1:T(8,128)}, u32[]{:S(2)}, u32[]{:S(2)}) collective-permute-start(f32[32,2,8,64]{0,3,2,1:T(8,128)} %get-tuple-element.10), channel_id=1, source_target_pairs={{0,13},{1,12},{2,15},{3,14},{4,9},{5,8},{6,11},{7,10},{8,5},{9,4},... | collective-permute-start | bytes 393224 | tf_op jit(solution)/shard_map/ppermute | solution.py:22
  128.3 78.8 %collective-permute-start.13 = (f32[32,2,8,64]{0,3,2,1:T(8,128)}, f32[32,2,8,64]{0,3,2,1:T(8,128)}, u32[]{:S(2)}, u32[]{:S(2)}) collective-permute-start(f32[32,2,8,64]{0,3,2,1:T(8,128)} %get-tuple-element.9), channel_id=1, source_target_pairs={{0,14},{1,15},{2,12},{3,13},{4,10},{5,11},{6,8},{7,9},{8,6},{9,7},... | collective-permute-start | bytes 393224 | tf_op jit(solution)/shard_map/ppermute | solution.py:22
  151.6 66.7 %collective-permute-start.14 = (f32[32,2,8,64]{0,3,2,1:T(8,128)}, f32[32,2,8,64]{0,3,2,1:T(8,128)S(1)}, u32[]{:S(2)}, u32[]{:S(2)}) collective-permute-start(f32[32,2,8,64]{0,3,2,1:T(8,128)} %get-tuple-element.8), channel_id=1, source_target_pairs={{0,15},{1,14},{2,13},{3,12},{4,11},{5,10},{6,9},{7,8},{8,7},{9,6},... | collective-permute-start | bytes 393224 | tf_op jit(solution)/shard_map/ppermute | solution.py:22
  220.3 25.7 %all-to-all-start = ((f32[32,2,8,1024]{3,0,1,2:T(8,128)}), f32[32,2,8,1024]{3,0,1,2:T(8,128)}, u32[]{:S(2)}, u32[]{:S(2)}) async-start(f32[32,2,8,1024]{3,0,1,2:T(8,128)} %dynamic_update_slice.63), calls=%async_computation | async-start | bytes 4194304 | tf_op jit(solution)/shard_map/all_to_all | solution.py:115
  246.1 57.0 %all-to-all-start.1 = ((f32[16,1,32768]{2,1,0:T(1,128)}), f32[16,1,32768]{2,1,0:T(1,128)}, u32[]{:S(2)}, u32[]{:S(2)}) async-start(f32[16,1,32768]{2,1,0:T(1,128)} %reshape.197), calls=%async_computation.1 | async-start | bytes 4194304 | tf_op jit(solution)/shard_map/all_to_all | solution.py:108
  303.1 52.4 %all-to-all-start.3 = ((f32[16,1,32768]{2,1,0:T(1,128)}), f32[16,1,32768]{2,1,0:T(1,128)}, u32[]{:S(2)}, u32[]{:S(2)}) async-start(f32[16,1,32768]{2,1,0:T(1,128)} %reshape.193), calls=%async_computation.3 | async-start | bytes 4194304 | tf_op jit(solution)/shard_map/all_to_all | solution.py:110
  322.4 38.6 %copy-start.23 = (f32[3,32,2048]{2,1,0:T(8,128)S(1)}, f32[3,32,2048]{2,1,0:T(8,128)}, u32[]{:S(2)}) copy-start(f32[3,32,2048]{2,1,0:T(8,128)} %param.15) | copy-start | bytes 2359300
  355.6 52.8 %all-to-all-start.5 = ((f32[16,1,32768]{2,1,0:T(1,128)}), f32[16,1,32768]{2,1,0:T(1,128)}, u32[]{:S(2)}, u32[]{:S(2)}) async-start(f32[16,1,32768]{2,1,0:T(1,128)} %reshape.195), calls=%async_computation.5 | async-start | bytes 4194304 | tf_op jit(solution)/shard_map/all_to_all | solution.py:111
  391.1 24.9 %copy-start.22 = (f32[32,16,128]{2,1,0:T(8,128)S(1)}, f32[32,16,128]{2,1,0:T(8,128)}, u32[]{:S(2)}) copy-start(f32[32,16,128]{2,1,0:T(8,128)} %copy.138) | copy-start | bytes 786436
  408.4 58.3 %all-to-all-start.2 = ((f32[32,2,8,1024]{3,1,0,2:T(2,128)}), f32[32,2,8,1024]{3,1,0,2:T(2,128)}, u32[]{:S(2)}, u32[]{:S(2)}) async-start(f32[32,2,8,1024]{3,1,0,2:T(2,128)} %reshape.190), calls=%async_computation.2 | async-start | bytes 4194304 | tf_op jit(solution)/shard_map/all_to_all | solution.py:114
  466.6 29.0 %all-to-all-start.4 = ((f32[32,2,8,1024]{3,1,0,2:T(2,128)}), f32[32,2,8,1024]{3,1,0,2:T(2,128)}, u32[]{:S(2)}, u32[]{:S(2)}) async-start(f32[32,2,8,1024]{3,1,0,2:T(2,128)} %reshape.191), calls=%async_computation.4 | async-start | bytes 4194304 | tf_op jit(solution)/shard_map/all_to_all | solution.py:116
  495.7 30.2 %all-to-all-start.6 = ((f32[32,2,8,1024]{3,1,0,2:T(2,128)}), f32[32,2,8,1024]{3,1,0,2:T(2,128)}, u32[]{:S(2)}, u32[]{:S(2)}) async-start(f32[32,2,8,1024]{3,1,0,2:T(2,128)} %reshape.192), calls=%async_computation.6 | async-start | bytes 4194304 | tf_op jit(solution)/shard_map/all_to_all | solution.py:117
  598.6 27.4 %all-to-all-start.7 = ((f32[2,1,262144]{2,1,0:T(1,128)}), f32[2,1,262144]{2,1,0:T(1,128)}, u32[]{:S(2)}, u32[]{:S(2)}) async-start(f32[2,1,262144]{2,1,0:T(1,128)} %reshape.203), calls=%async_computation.7 | async-start | bytes 4194304 | tf_op jit(solution)/shard_map/all_to_all | solution.py:158
  626.0 47.6 %all-to-all-start.9 = ((f32[2,1,262144]{2,1,0:T(1,128)}), f32[2,1,262144]{2,1,0:T(1,128)}, u32[]{:S(2)}, u32[]{:S(2)}) async-start(f32[2,1,262144]{2,1,0:T(1,128)} %reshape.199), calls=%async_computation.9 | async-start | bytes 4194304 | tf_op jit(solution)/shard_map/all_to_all | solution.py:165
  673.6 55.1 %all-to-all-start.8 = ((f32[16,1,32768]{2,1,0:T(1,128)}), f32[16,1,32768]{2,1,0:T(1,128)}, u32[]{:S(2)}, u32[]{:S(2)}) async-start(f32[16,1,32768]{2,1,0:T(1,128)} %reshape.205), calls=%async_computation.8 | async-start | bytes 4194304 | tf_op jit(solution)/shard_map/all_to_all | solution.py:157
  728.7 52.6 %all-to-all-start.10 = ((f32[16,1,32768]{2,1,0:T(1,128)}), f32[16,1,32768]{2,1,0:T(1,128)}, u32[]{:S(2)}, u32[]{:S(2)}) async-start(f32[16,1,32768]{2,1,0:T(1,128)} %reshape.201), calls=%async_computation.10 | async-start | bytes 4194304 | tf_op jit(solution)/shard_map/all_to_all | solution.py:164
  (35 other events, 212.8 us)
